TPU v7x, 32 devices: a whole 2x2x4 slice. The times are simulated.
32 devices in a mesh: gx: 4 (over y, x), gy: 8 (over z, core).
Axes of the slice: x: 2, y: 2, z: 4, core: 2. Of those that a mesh axis runs over, the one named last changes fastest.
Arguments:
- traces: bfloat16 [2048, 1024], P(('gx', 'gy')), may hold values from -6 to 6
- filter_taps: float32 [8], replicated, may hold values from -3 to 3
- aperture: int32 [2048, 8], P(('gx', 'gy')), may hold values from 0 to 31, all different within a row; in each aligned block of 64 rows (0 to 63, 64 to 127, ...) at most 32 rows name the same one
- midpoint: int32 [2048, 8], P(('gx', 'gy')), may hold values from 0 to 287
- time_index: int32 [128, 64], replicated, may hold values from 0 to 1022
- time_frac: float32 [128, 64], replicated, may hold values from 0 to 1
- amplitude: float32 [128, 64], replicated, may hold values from 0.02 to 0.2
Outputs:
- image: float32 [16, 4096], P('gx', 'gy')
Inputs may be any that keep to these rules, and one draw needn't show every extreme that they name: `aperture`: each trace names 8 different tiles; among the rows of one device no tile is named by more than 32 rows, a bound that some block reaches.
All inputs are finite; a program needn't handle non-finite values.
Results may differ from a plain program's by a relative error of at most 0.005.
Values may be sent and summed in bfloat16 or wider, within the bound.
A program may use at most 64 MiB of HBM per device.

v0:
```python
import jax
import jax.numpy as jnp
from jax import lax
from jax.sharding import PartitionSpec as P

TX = 4
TY = 8


def with_halo(cells, sides, width):
    for axis, dim in sides:
        count = lax.axis_size(axis)
        ends = count - 1
        head = lax.slice_in_dim(cells, 0, width, axis=dim)
        tail = lax.slice_in_dim(cells, cells.shape[dim] - width, cells.shape[dim], axis=dim)
        cells = jnp.concatenate(
            [
                lax.ppermute(tail, axis, [(i, (i + 1) % count) for i in range(ends)]),
                cells,
                lax.ppermute(head, axis, [((i + 1) % count, i) for i in range(ends)]),
            ],
            axis=dim,
        )
    return cells


def fir_filter(traces, filter_taps):
    samples = traces.shape[1]
    taps_count = filter_taps.shape[0]
    padded = jnp.pad(traces.astype(jnp.float32), ((0, 0), (taps_count - 1, 0)))
    total = jnp.zeros(traces.shape, jnp.float32)
    for offset in range(taps_count):
        total = (
            total
            + filter_taps[offset]
            * padded[:, taps_count - 1 - offset : taps_count - 1 - offset + samples]
        )
    return total.astype(jnp.bfloat16)


def distance_bins(mid_row, mid_col):
    points = jnp.arange(TX * TY, dtype=jnp.int32)
    across = points // TY
    along = points % TY
    return jnp.abs(mid_row[:, None] - TX - across[None, :]) * (2 * TY) + jnp.abs(
        mid_col[:, None] - TY - along[None, :]
    )


def body(traces, filter_taps, aperture, midpoint, time_index, time_frac, amplitude):
    trace_rows, samples = traces.shape
    entries = aperture.shape[1]
    rows_inline = lax.axis_size("gx")
    rows_cross = lax.axis_size("gy")
    tile_count = rows_inline * rows_cross
    capacity = 2 * trace_rows * entries // tile_count
    slot_count = capacity * tile_count
    depth = time_frac.shape[1]
    table_rows = time_frac.shape[0]
    points = TX * TY
    filtered = fir_filter(traces, filter_taps)
    target = aperture.reshape(-1)
    marks = (target[:, None] == jnp.arange(tile_count, dtype=jnp.int32)[None, :]).astype(jnp.int32)
    before = jnp.sum(jnp.cumsum(marks, axis=0) * marks, axis=1) - 1
    slot_index = target * capacity + before
    placing = jnp.arange(slot_count, dtype=jnp.int32)[:, None] == slot_index[None, :]
    chooser = jnp.sum(
        placing.reshape(slot_count, trace_rows, entries).astype(jnp.int32), axis=2
    ).astype(jnp.bfloat16)
    outgoing = jnp.dot(chooser, filtered, preferred_element_type=jnp.float32).astype(jnp.bfloat16)
    mid_flat = midpoint.reshape(-1)
    mid_pairs = jnp.stack([mid_flat // (3 * TY), mid_flat % (3 * TY)], axis=1)
    outgoing_pairs = jnp.sum(
        jnp.where(placing[:, :, None], mid_pairs[None, :, :], 0), axis=1
    ).astype(jnp.bfloat16)
    received, received_pairs = (
        lax.all_to_all(outgoing, ("gx", "gy"), split_axis=0, concat_axis=0, tiled=True),
        lax.all_to_all(outgoing_pairs, ("gx", "gy"), split_axis=0, concat_axis=0, tiled=True),
    )
    pair_ints = received_pairs.astype(jnp.int32)
    bins = distance_bins(pair_ints[:, 0], pair_ints[:, 1])
    low_whole = (1.0 - time_frac).astype(jnp.bfloat16)
    high_whole = time_frac.astype(jnp.bfloat16)
    block_bins = 16
    sample_axis = jnp.arange(samples, dtype=jnp.int32)[:, None, None]

    def add_rows(turn, image):
        start = turn * block_bins
        index_rows = lax.dynamic_slice_in_dim(time_index, start, block_bins, 0)
        low = lax.dynamic_slice_in_dim(low_whole, start, block_bins, 0)
        high = lax.dynamic_slice_in_dim(high_whole, start, block_bins, 0)
        amp_rows = lax.dynamic_slice_in_dim(amplitude, start, block_bins, 0)
        weights = jnp.where(
            sample_axis == index_rows[None],
            low[None],
            jnp.where(sample_axis == index_rows[None] + 1, high[None], jnp.zeros((), jnp.bfloat16)),
        )
        values = jnp.dot(
            received,
            weights.reshape(samples, block_bins * depth),
            preferred_element_type=jnp.float32,
        )
        scaled = (values.reshape(slot_count, block_bins, depth) * amp_rows[None]).astype(
            jnp.bfloat16
        )
        picks = (
            bins[:, :, None] == start + jnp.arange(block_bins, dtype=jnp.int32)[None, None, :]
        ).astype(jnp.bfloat16)
        return image + jnp.einsum("jpr,jrz->pz", picks, scaled, preferred_element_type=jnp.float32)

    image = lax.fori_loop(
        0, table_rows // block_bins, add_rows, jnp.zeros((points, depth), jnp.float32)
    )
    raw = image.reshape(TX, TY, depth)
    padded = with_halo(raw, (("gx", 0), ("gy", 1)), 1)
    beside = padded[2:, 1:-1] + padded[:-2, 1:-1] + padded[1:-1, 2:] + padded[1:-1, :-2]
    smooth = raw + 0.25 * beside
    return smooth.reshape(TX, TY * depth)


def solution(mesh):
    in_specs = (
        P(("gx", "gy"), None),
        P(),
        P(("gx", "gy"), None),
        P(("gx", "gy"), None),
        P(),
        P(),
        P(),
    )
    out_specs = P("gx", "gy")
    return jax.shard_map(body, mesh=mesh, in_specs=in_specs, out_specs=out_specs, check_vma=False)
```

profile of v0, /device:TPU:0, one launch (start us, length us, event | category | flops | bytes accessed | tf_op | source)
XLA Modules:
  0.0 123.0 jit_solution(15333356782674116741)
XLA Ops:
  3.0 1.2 reduce-window.6
  6.3 7.3 %all-to-all-start = ((bf16[32,32,2]{1,2,0:T(2,128)(2,1)}), bf16[32,32,2]{1,2,0:T(2,128)(2,1)S(1)}, u32[]{:S(2)}, u32[]{:S(2)}) async-start(bf16[32,32,2]{1,2,0:T(2,128)(2,1)} %copy.77), calls=%async_computation | async-start | bytes 32768 | tf_op jit(solution)/shard_map/all_to_all | solution.py:78
  13.6 1.6 %fusion.60 = (f32[1]{0:T(128)}, f32[1]{0:T(128)}, f32[1]{0:T(128)}, f32[1]{0:T(128)}, f32[1]{0:T(128)}, /*index=5*/f32[1]{0:T(128)}, f32[1]{0:T(128)}, f32[1]{0:T(128)}) fusion(f32[8]{0:T(128)} %param.10), kind=kLoop, calls=%fused_computation.110 | loop fusion | bytes 64 | tf_op jit(solution)/shard_map/slice | solution.py:35
  16.9 7.5 %convolution_convert_fusion = bf16[1024,1024]{1,0:T(8,128)(2,1)} fusion(f32[64,1024]{1,0:T(8,128)S(1)} %convert_element_type.60, f32[]{:T(128)} %bitcast.8, f32[]{:T(128)} %bitcast.7, f32[]{:T(128)} %bitcast.6, f32[]{:T(128)} %bitcast.5, f32[]{:T(128)} %bitcast.4, f32[]{:T(128)} %bitcast.3, f32[]{:T(128)} %bitcast.2, f32[]{:T(128)} %bitcast.1, ...), kind=kOutput, calls=%fused_computation.32 | convolution fusion | flops 136380416 | bytes 2621472 | tf_op jit(solution)/shard_map/dot_general | solution.py:70
  24.5 5.8 %all-to-all-start.1 = ((bf16[32,32,1024]{2,1,0:T(8,128)(2,1)}), bf16[32,32,1024]{2,1,0:T(8,128)(2,1)S(1)}, u32[]{:S(2)}, u32[]{:S(2)}) async-start(bf16[32,32,1024]{2,1,0:T(8,128)(2,1)} %bitcast.9), calls=%async_computation.1 | async-start | bytes 4194304 | tf_op jit(solution)/shard_map/all_to_all | solution.py:77
  30.8 49.6 %all-to-all-done.1 = bf16[32,32,1024]{2,1,0:T(8,128)(2,1)S(1)} async-done(((bf16[32,32,1024]{2,1,0:T(8,128)(2,1)}), bf16[32,32,1024]{2,1,0:T(8,128)(2,1)S(1)}, u32[]{:S(2)}, u32[]{:S(2)}) %all-to-all-start.1) | async-done | bytes 2097184 | tf_op jit(solution)/shard_map/all_to_all | solution.py:77
  80.4 29.3 %while.15 = (s32[]{:T(128)}, f32[32,64]{1,0:T(8,128)S(1)}, s32[128,64]{1,0:T(8,128)S(1)}, bf16[128,64]{1,0:T(8,128)(2,1)S(1)}, bf16[128,64]{1,0:T(8,128)(2,1)S(1...) while((s32[]{:T(128)}, f32[32,64]{1,0:T(8,128)S(1)}, ...), condition=%wide.region_6.7_spmd.clone.clone, body=%wide.region_5.6_spmd.clone.clone.sunk | while | flops 2221609984 | bytes 10842717 | solution.py:111
  80.9 2.4 %fusion.70 = f32[1024,1024]{1,0:T(8,128)S(1)} fusion(bf16[1024,1024]{1,0:T(8,128)(2,1)S(1)} %get-tuple-element.455, s32[1024]{0:T(1024)S(1)} %eq.262, s32[1024]{0:T(1024)S(1)} %eq.263, bf16[1024]{0:T(1024)(128)(2,1)S(1)} %broadcast_in_dim.125, bf16[1024]{0:T(1024)(128)(2,1)S(1)} %broadcast_in_dim.126), kind=kOutput, calls=%fused_computation.7.clone.1 | convolution fusion | flops 2151677952 | bytes 6303744 | tf_op jit(solution)/shard_map/while/body/eval_jaxpr/dot_general | solution.py:98
  84.5 2.4 %fusion.70 = f32[1024,1024]{1,0:T(8,128)S(1)} fusion(bf16[1024,1024]{1,0:T(8,128)(2,1)S(1)} %get-tuple-element.455, s32[1024]{0:T(1024)S(1)} %eq.262, s32[1024]{0:T(1024)S(1)} %eq.263, bf16[1024]{0:T(1024)(128)(2,1)S(1)} %broadcast_in_dim.125, bf16[1024]{0:T(1024)(128)(2,1)S(1)} %broadcast_in_dim.126), kind=kOutput, calls=%fused_computation.7.clone.1 | convolution fusion | flops 2151677952 | bytes 6303744 | tf_op jit(solution)/shard_map/while/body/eval_jaxpr/dot_general | solution.py:98
  86.9 0.8 fusion.71
  88.2 2.4 %fusion.70 = f32[1024,1024]{1,0:T(8,128)S(1)} fusion(bf16[1024,1024]{1,0:T(8,128)(2,1)S(1)} %get-tuple-element.455, s32[1024]{0:T(1024)S(1)} %eq.262, s32[1024]{0:T(1024)S(1)} %eq.263, bf16[1024]{0:T(1024)(128)(2,1)S(1)} %broadcast_in_dim.125, bf16[1024]{0:T(1024)(128)(2,1)S(1)} %broadcast_in_dim.126), kind=kOutput, calls=%fused_computation.7.clone.1 | convolution fusion | flops 2151677952 | bytes 6303744 | tf_op jit(solution)/shard_map/while/body/eval_jaxpr/dot_general | solution.py:98
  90.6 0.8 fusion.71
  91.9 2.4 %fusion.70 = f32[1024,1024]{1,0:T(8,128)S(1)} fusion(bf16[1024,1024]{1,0:T(8,128)(2,1)S(1)} %get-tuple-element.455, s32[1024]{0:T(1024)S(1)} %eq.262, s32[1024]{0:T(1024)S(1)} %eq.263, bf16[1024]{0:T(1024)(128)(2,1)S(1)} %broadcast_in_dim.125, bf16[1024]{0:T(1024)(128)(2,1)S(1)} %broadcast_in_dim.126), kind=kOutput, calls=%fused_computation.7.clone.1 | convolution fusion | flops 2151677952 | bytes 6303744 | tf_op jit(solution)/shard_map/while/body/eval_jaxpr/dot_general | solution.py:98
  94.3 0.8 fusion.71
  95.6 2.4 %fusion.70 = f32[1024,1024]{1,0:T(8,128)S(1)} fusion(bf16[1024,1024]{1,0:T(8,128)(2,1)S(1)} %get-tuple-element.455, s32[1024]{0:T(1024)S(1)} %eq.262, s32[1024]{0:T(1024)S(1)} %eq.263, bf16[1024]{0:T(1024)(128)(2,1)S(1)} %broadcast_in_dim.125, bf16[1024]{0:T(1024)(128)(2,1)S(1)} %broadcast_in_dim.126), kind=kOutput, calls=%fused_computation.7.clone.1 | convolution fusion | flops 2151677952 | bytes 6303744 | tf_op jit(solution)/shard_map/while/body/eval_jaxpr/dot_general | solution.py:98
  99.2 2.4 %fusion.70 = f32[1024,1024]{1,0:T(8,128)S(1)} fusion(bf16[1024,1024]{1,0:T(8,128)(2,1)S(1)} %get-tuple-element.455, s32[1024]{0:T(1024)S(1)} %eq.262, s32[1024]{0:T(1024)S(1)} %eq.263, bf16[1024]{0:T(1024)(128)(2,1)S(1)} %broadcast_in_dim.125, bf16[1024]{0:T(1024)(128)(2,1)S(1)} %broadcast_in_dim.126), kind=kOutput, calls=%fused_computation.7.clone.1 | convolution fusion | flops 2151677952 | bytes 6303744 | tf_op jit(solution)/shard_map/while/body/eval_jaxpr/dot_general | solution.py:98
  102.9 2.4 %fusion.70 = f32[1024,1024]{1,0:T(8,128)S(1)} fusion(bf16[1024,1024]{1,0:T(8,128)(2,1)S(1)} %get-tuple-element.455, s32[1024]{0:T(1024)S(1)} %eq.262, s32[1024]{0:T(1024)S(1)} %eq.263, bf16[1024]{0:T(1024)(128)(2,1)S(1)} %broadcast_in_dim.125, bf16[1024]{0:T(1024)(128)(2,1)S(1)} %broadcast_in_dim.126), kind=kOutput, calls=%fused_computation.7.clone.1 | convolution fusion | flops 2151677952 | bytes 6303744 | tf_op jit(solution)/shard_map/while/body/eval_jaxpr/dot_general | solution.py:98
  106.6 2.4 %fusion.70 = f32[1024,1024]{1,0:T(8,128)S(1)} fusion(bf16[1024,1024]{1,0:T(8,128)(2,1)S(1)} %get-tuple-element.455, s32[1024]{0:T(1024)S(1)} %eq.262, s32[1024]{0:T(1024)S(1)} %eq.263, bf16[1024]{0:T(1024)(128)(2,1)S(1)} %broadcast_in_dim.125, bf16[1024]{0:T(1024)(128)(2,1)S(1)} %broadcast_in_dim.126), kind=kOutput, calls=%fused_computation.7.clone.1 | convolution fusion | flops 2151677952 | bytes 6303744 | tf_op jit(solution)/shard_map/while/body/eval_jaxpr/dot_general | solution.py:98
  109.8 1.6 %collective-permute-start.1 = (f32[1,8,64]{2,1,0:T(8,128)S(1)}, f32[1,8,64]{2,1,0:T(8,128)S(1)}, u32[]{:S(2)}, u32[]{:S(2)}) collective-permute-start(f32[1,8,64]{2,1,0:T(8,128)S(1)} %get-tuple-element.325), channel_id=1, source_target_pairs={{0,8},{8,16},{16,24},{1,9},{9,17},{17,25},{2,10},{10,18},{18,26},{... | collective-permute-start | bytes 6152 | tf_op jit(solution)/shard_map/ppermute | solution.py:18
  111.4 1.3 %collective-permute-start = (f32[1,8,64]{2,1,0:T(8,128)S(1)}, f32[1,8,64]{2,1,0:T(8,128)S(1)}, u32[]{:S(2)}, u32[]{:S(2)}) collective-permute-start(f32[1,8,64]{2,1,0:T(8,128)S(1)} %get-tuple-element.326), channel_id=1, source_target_pairs={{8,0},{16,8},{24,16},{9,1},{17,9},{25,17},{10,2},{18,10},{26,18},{... | collective-permute-start | bytes 6152 | tf_op jit(solution)/shard_map/ppermute | solution.py:20
  112.7 4.5 %collective-permute-done = f32[1,8,64]{2,1,0:T(8,128)S(1)} collective-permute-done((f32[1,8,64]{2,1,0:T(8,128)S(1)}, f32[1,8,64]{2,1,0:T(8,128)S(1)}, u32[]{:S(2)}, u32[]{:S(2)}) %collective-permute-start) | collective-permute-done | bytes 2080 | tf_op jit(solution)/shard_map/ppermute | solution.py:20
  117.2 1.3 %collective-permute-start.2 = (f32[6,1,64]{2,1,0:T(1,128)S(1)}, f32[6,1,64]{2,1,0:T(1,128)S(1)}, u32[]{:S(2)}, u32[]{:S(2)}) collective-permute-start(f32[6,1,64]{2,1,0:T(1,128)S(1)} %get-tuple-element.323), channel_id=1, source_target_pairs={{1,0},{2,1},{3,2},{4,3},{5,4},{6,5},{7,6},{9,8},{10,9},{11,10},{12... | collective-permute-start | bytes 4616 | tf_op jit(solution)/shard_map/ppermute | solution.py:20
  118.5 3.0 %collective-permute-start.3 = (f32[6,1,64]{2,1,0:T(1,128)S(1)}, f32[6,1,64]{2,1,0:T(1,128)S(1)}, u32[]{:S(2)}, u32[]{:S(2)}) collective-permute-start(f32[6,1,64]{2,1,0:T(1,128)S(1)} %get-tuple-element.324), channel_id=1, source_target_pairs={{0,1},{1,2},{2,3},{3,4},{4,5},{5,6},{6,7},{8,9},{9,10},{10,11},{11... | collective-permute-start | bytes 4616 | tf_op jit(solution)/shard_map/ppermute | solution.py:18
  121.5 0.8 collective-permute-done.3
  (131 shorter events, 15.3 us)
Async XLA Ops:
  0.0 16.9 %copy-start = (bf16[64,1024]{1,0:T(8,128)(2,1)S(1)}, bf16[64,1024]{1,0:T(8,128)(2,1)}, u32[]{:S(2)}) copy-start(bf16[64,1024]{1,0:T(8,128)(2,1)} %param.9) | copy-start | bytes 393220
  6.3 18.1 %all-to-all-start = ((bf16[32,32,2]{1,2,0:T(2,128)(2,1)}), bf16[32,32,2]{1,2,0:T(2,128)(2,1)S(1)}, u32[]{:S(2)}, u32[]{:S(2)}) async-start(bf16[32,32,2]{1,2,0:T(2,128)(2,1)} %copy.77), calls=%async_computation | async-start | bytes 32768 | tf_op jit(solution)/shard_map/all_to_all | solution.py:78
  24.5 5.9 %copy-start.1 = (s32[128,64]{0,1:T(8,128)S(1)}, s32[128,64]{0,1:T(8,128)}, u32[]{:S(2)}) copy-start(s32[128,64]{0,1:T(8,128)} %param.13) | copy-start | bytes 98308
  24.5 6.0 %copy-start.2 = (f32[128,64]{0,1:T(8,128)S(1)}, f32[128,64]{0,1:T(8,128)}, u32[]{:S(2)}) copy-start(f32[128,64]{0,1:T(8,128)} %param.14) | copy-start | bytes 98308
  24.5 6.1 %copy-start.3 = (f32[128,64]{0,1:T(8,128)S(1)}, f32[128,64]{0,1:T(8,128)}, u32[]{:S(2)}) copy-start(f32[128,64]{0,1:T(8,128)} %param.15) | copy-start | bytes 98308
  24.5 56.0 %all-to-all-start.1 = ((bf16[32,32,1024]{2,1,0:T(8,128)(2,1)}), bf16[32,32,1024]{2,1,0:T(8,128)(2,1)S(1)}, u32[]{:S(2)}, u32[]{:S(2)}) async-start(bf16[32,32,1024]{2,1,0:T(8,128)(2,1)} %bitcast.9), calls=%async_computation.1 | async-start | bytes 4194304 | tf_op jit(solution)/shard_map/all_to_all | solution.py:77
  109.8 2.9 %collective-permute-start.1 = (f32[1,8,64]{2,1,0:T(8,128)S(1)}, f32[1,8,64]{2,1,0:T(8,128)S(1)}, u32[]{:S(2)}, u32[]{:S(2)}) collective-permute-start(f32[1,8,64]{2,1,0:T(8,128)S(1)} %get-tuple-element.325), channel_id=1, source_target_pairs={{0,8},{8,16},{16,24},{1,9},{9,17},{17,25},{2,10},{10,18},{18,26},{... | collective-permute-start | bytes 6152 | tf_op jit(solution)/shard_map/ppermute | solution.py:18
  111.4 5.8 %collective-permute-start = (f32[1,8,64]{2,1,0:T(8,128)S(1)}, f32[1,8,64]{2,1,0:T(8,128)S(1)}, u32[]{:S(2)}, u32[]{:S(2)}) collective-permute-start(f32[1,8,64]{2,1,0:T(8,128)S(1)} %get-tuple-element.326), channel_id=1, source_target_pairs={{8,0},{16,8},{24,16},{9,1},{17,9},{25,17},{10,2},{18,10},{26,18},{... | collective-permute-start | bytes 6152 | tf_op jit(solution)/shard_map/ppermute | solution.py:20
  117.2 4.3 %collective-permute-start.2 = (f32[6,1,64]{2,1,0:T(1,128)S(1)}, f32[6,1,64]{2,1,0:T(1,128)S(1)}, u32[]{:S(2)}, u32[]{:S(2)}) collective-permute-start(f32[6,1,64]{2,1,0:T(1,128)S(1)} %get-tuple-element.323), channel_id=1, source_target_pairs={{1,0},{2,1},{3,2},{4,3},{5,4},{6,5},{7,6},{9,8},{10,9},{11,10},{12... | collective-permute-start | bytes 4616 | tf_op jit(solution)/shard_map/ppermute | solution.py:20
  118.5 3.8 %collective-permute-start.3 = (f32[6,1,64]{2,1,0:T(1,128)S(1)}, f32[6,1,64]{2,1,0:T(1,128)S(1)}, u32[]{:S(2)}, u32[]{:S(2)}) collective-permute-start(f32[6,1,64]{2,1,0:T(1,128)S(1)} %get-tuple-element.324), channel_id=1, source_target_pairs={{0,1},{1,2},{2,3},{3,4},{4,5},{5,6},{6,7},{8,9},{9,10},{10,11},{11... | collective-permute-start | bytes 4616 | tf_op jit(solution)/shard_map/ppermute | solution.py:18
where the time goes:
time: 124 us; the launch traced here: 123 us
  waiting for transfers between devices  54.9 us (44%)
  matrix products  32.8 us (26%)
  starting transfers between devices  20.4 us (16%)
  local copies, waits for them, and re-layouts  7.96 us (6%)
  other arithmetic  6.23 us (5%)
    all_to_all x1, waiting for transfers between devices, body(): lax.all_to_all(outgoing, ('gx', 'gy'), split_axis=0, concat_axis=0, tiled...  49.6 us
    dot_general x8, matrix products, add_rows(): jnp.dot(received, weights.reshape(samples, block_bins * depth), preferred...  19.1 us
    dot_general x1, matrix products, body(): jnp.dot(chooser, filtered, preferred_element_type=jnp.float32)  7.54 us
    all_to_all x1, starting transfers between devices, body(): lax.all_to_all(outgoing_pairs, ('gx', 'gy'), split_axis=0, concat_axis=0,...  7.3 us
    dot_general x8, matrix products, add_rows(): jnp.einsum('jpr,jrz->pz', picks, scaled, preferred_element_type=jnp.float32)  6.18 us
    all_to_all x1, starting transfers between devices, body(): lax.all_to_all(outgoing, ('gx', 'gy'), split_axis=0, concat_axis=0, tiled...  5.84 us
    ppermute x2, starting transfers between devices, with_halo(): lax.ppermute(tail, axis, [(i, (i + 1) % count) for i in range(ends)])  4.63 us
    ppermute x2, waiting for transfers between devices, with_halo(): lax.ppermute(head, axis, [((i + 1) % count, i) for i in range(ends)])  4.5 us
  transfers between devices with their start and end apart: 6, of which 3 were waited for; matrix products, arithmetic and copies ran while one was open for 9% of the time, Pallas kernels for 0%

commit v1 on v0

v1 whole, which is shorter than its diff:
```python
import functools

import jax
import jax.numpy as jnp
from jax import lax
from jax.experimental import pallas as pl
from jax.experimental.pallas import tpu as pltpu
from jax.sharding import PartitionSpec as P

TX = 4
TY = 8
MESH = pl.DeviceIdType.MESH
WINDOW = 256
PAIRS = 14
FLAT = 32
STRIDE = PAIRS * FLAT


def local_kernel(
    ngx, ngy, taps_ref, ap_ref, mid_ref, tr_ref, ti_ref, tf_ref, am_ref, out_ref,
    f4_ref, idx_ref, low_ref, high_ref, amp_ref, tab_ref, img_ref,
):
    f32, bf16 = jnp.float32, jnp.bfloat16
    rows, samples = tr_ref.shape
    taps_count = taps_ref.shape[0]
    entries = ap_ref.shape[1]
    windows = samples // WINDOW
    span = 2 * TY
    cols = idx_ref.shape[1]
    pitch = ngy * TY + 16

    x = tr_ref[...].astype(f32)
    lane = lax.broadcasted_iota(jnp.int32, (rows, samples), 1)
    total = jnp.zeros((rows, samples), f32)
    for k in range(taps_count):
        moved = x if k == 0 else jnp.where(lane < k, 0.0, pltpu.roll(x, k, 1))
        total = total + taps_ref[k] * moved
    filtered = total.astype(bf16)
    for j in range(windows):
        f4_ref[j * rows : (j + 1) * rows, :] = filtered[:, j * WINDOW : (j + 1) * WINDOW]
    rounded = filtered.astype(f32)
    edges = [rounded[:, j * WINDOW : j * WINDOW + 1] for j in range(1, windows)]

    for m in range(TX):
        def side(ref):
            return jnp.concatenate(
                [ref[(2 * m) * span : (2 * m + 1) * span, :], ref[(2 * m + 1) * span : (2 * m + 2) * span, :]],
                axis=1,
            )

        here = slice(m * 128, (m + 1) * 128)
        frac = side(tf_ref)
        idx_ref[:, here] = side(ti_ref)
        low_ref[:, here] = (1.0 - frac).astype(bf16).astype(f32)
        high_ref[:, here] = frac.astype(bf16).astype(f32)
        amp_ref[:, here] = side(am_ref)

    first = lax.broadcasted_iota(jnp.int32, (rows, 128), 1) < 64

    def per_distance(b, carry):
        idx = idx_ref[pl.ds(b, 1), :]
        low = low_ref[pl.ds(b, 1), :]
        high = high_ref[pl.ds(b, 1), :]
        amp = amp_ref[pl.ds(b, 1), :]
        inside = idx & (WINDOW - 1)
        window = idx >> 8
        q = jnp.broadcast_to(inside.astype(f32), (16, cols)).astype(bf16)
        lowb = jnp.broadcast_to(low, (16, cols)).astype(bf16)
        highb = jnp.broadcast_to(high, (16, cols)).astype(bf16)
        q1 = q + jnp.ones((), bf16)
        at = lax.broadcasted_iota(jnp.int32, (16, cols), 0).astype(f32).astype(bf16)
        zero = jnp.zeros((16, cols), bf16)
        blocks = []
        for i in range(WINDOW // 16):
            here = at + jnp.asarray(16 * i, bf16)
            blocks.append(jnp.where(here == q, lowb, jnp.where(here == q1, highb, zero)))
        weights = jnp.concatenate(blocks, axis=0)
        products = jnp.dot(f4_ref[...], weights, preferred_element_type=f32)
        over = jnp.where(inside == WINDOW - 1, high, 0.0)
        value = products[(windows - 1) * rows :]
        edge = jnp.broadcast_to(edges[windows - 2], (rows, cols))
        for j in range(windows - 2, -1, -1):
            value = jnp.where(window == j, products[j * rows : (j + 1) * rows], value)
            if j < windows - 2:
                edge = jnp.where(window == j, jnp.broadcast_to(edges[j], (rows, cols)), edge)
        value = value + over * edge
        sample = (amp * value).astype(bf16).astype(f32)
        own = [sample[:, m * 128 : (m + 1) * 128] for m in range(TX)]
        swapped = [pltpu.roll(s, 64, 1) for s in own]

        def put(offset, block):
            start = (offset + 6) * FLAT + 15
            tab_ref[pl.ds(start - b, rows, stride=STRIDE), :] = block
            tab_ref[pl.ds(start + b, rows, stride=STRIDE), :] = block

        for m in range(TX):
            put(2 * m + 1, swapped[m])
            put(-2 * m, own[m])
            if m < TX - 1:
                put(2 * m + 2, jnp.where(first, own[m + 1], own[m]))
                put(-2 * m - 1, jnp.where(first, swapped[m], swapped[m + 1]))
        return carry

    lax.fori_loop(0, span, per_distance, 0)

    img_ref[...] = jnp.zeros_like(img_ref)

    def per_trace(t, carry):
        base = t * STRIDE + 23
        source, place = [], []
        for e in range(entries):
            m = mid_ref[t, e]
            tile = ap_ref[t, e]
            source.append(base - m + 56 * ((m * 2731) >> 16))
            place.append(
                pl.multiple_of(pitch + 8 + (tile // ngy) * (2 * pitch) + (tile % ngy) * TY, 8)
            )
        sums = []
        for e in range(entries):
            sums.append(img_ref[pl.ds(place[e], TY), :] + tab_ref[pl.ds(source[e] + 2 * FLAT, TY), :])
            sums.append(img_ref[pl.ds(place[e] + pitch, TY), :] + tab_ref[pl.ds(source[e], TY), :])
        for e in range(entries):
            img_ref[pl.ds(place[e], TY), :] = sums[2 * e]
            img_ref[pl.ds(place[e] + pitch, TY), :] = sums[2 * e + 1]
        return carry

    lax.fori_loop(0, rows, per_trace, 0)

    head = lax.broadcasted_iota(jnp.int32, (TY, 128), 1) < 64

    def per_tile(tile, carry):
        start = pl.multiple_of(pitch + 8 + (tile // ngy) * (2 * pitch) + (tile % ngy) * TY, 8)
        planes = [img_ref[pl.ds(start + (p - 1) * pitch, TY), :] for p in range(4)]
        parts = []
        for u in range(2):
            below, mid, above = planes[u], planes[u + 1], planes[u + 2]
            along = img_ref[pl.ds(start + u * pitch - 1, TY), :] + img_ref[pl.ds(start + u * pitch + 1, TY), :]
            across = pltpu.roll(jnp.where(head, above + mid, mid + below), 64, 1)
            parts.append(mid + 0.25 * (across + along))
        out_ref[tile] = jnp.concatenate(parts, axis=0).astype(bf16)
        return carry

    lax.fori_loop(0, ngx * ngy, per_tile, 0, unroll=4)


def exchange_kernel(count, ngy, part_ref, out_ref, held, send_sem, recv_sem):
    me = lax.axis_index("gx") * ngy + lax.axis_index("gy")

    def at(peer):
        return (peer // ngy, peer % ngy)

    barrier = pltpu.get_barrier_semaphore()

    def greet(step, carry):
        pl.semaphore_signal(barrier, inc=1, device_id=at((me + step) % count), device_id_type=MESH)
        return carry

    lax.fori_loop(1, count, greet, 0)
    pl.semaphore_wait(barrier, count - 1)

    def copy(step):
        peer = (me + step) % count
        return pltpu.make_async_remote_copy(
            src_ref=part_ref.at[peer],
            dst_ref=held.at[step],
            send_sem=send_sem.at[step],
            recv_sem=recv_sem.at[step],
            device_id=at(peer),
            device_id_type=MESH,
        )

    def send(step, carry):
        copy(step).start()
        return carry

    lax.fori_loop(1, count, send, 0)

    def take(step, total):
        copy(step).wait_recv()
        return total + held[step].astype(jnp.float32)

    total = lax.fori_loop(1, count, take, part_ref[me].astype(jnp.float32))
    out_ref[...] = total

    def done(step, carry):
        copy(step).wait_send()
        return carry

    lax.fori_loop(1, count, done, 0)


def body(ngx, ngy, traces, filter_taps, aperture, midpoint, time_index, time_frac, amplitude):
    rows, samples = traces.shape
    depth = time_frac.shape[1]
    count = ngx * ngy
    span = 2 * TY
    cols = 2 * TX * depth
    vmem = pl.BlockSpec(memory_space=pltpu.VMEM)
    smem = pl.BlockSpec(memory_space=pltpu.SMEM)
    parts = pl.pallas_call(
        functools.partial(local_kernel, ngx, ngy),
        out_shape=jax.ShapeDtypeStruct((count, 2 * TY, 2 * depth), jnp.bfloat16),
        in_specs=[smem, smem, smem, vmem, vmem, vmem, vmem],
        out_specs=vmem,
        scratch_shapes=[
            pltpu.VMEM((rows * samples // WINDOW, WINDOW), jnp.bfloat16),
            pltpu.VMEM((span, cols), jnp.int32),
            pltpu.VMEM((span, cols), jnp.float32),
            pltpu.VMEM((span, cols), jnp.float32),
            pltpu.VMEM((span, cols), jnp.float32),
            pltpu.VMEM((rows * STRIDE, 2 * depth), jnp.float32),
            pltpu.VMEM(((2 * ngx + 2) * (ngy * TY + 16), 2 * depth), jnp.float32),
        ],
        compiler_params=pltpu.CompilerParams(vmem_limit_bytes=40 * 1024 * 1024),
        name="migrate",
    )(filter_taps, aperture, midpoint, traces, time_index, time_frac, amplitude)
    image = pl.pallas_call(
        functools.partial(exchange_kernel, count, ngy),
        out_shape=jax.ShapeDtypeStruct((2 * TY, 2 * depth), jnp.float32),
        in_specs=[vmem],
        out_specs=vmem,
        scratch_shapes=[
            pltpu.VMEM((count, 2 * TY, 2 * depth), jnp.bfloat16),
            pltpu.SemaphoreType.DMA((count,)),
            pltpu.SemaphoreType.DMA((count,)),
        ],
        compiler_params=pltpu.CompilerParams(collective_id=0, has_side_effects=True),
        name="exchange",
    )(parts)
    return image.reshape(2, TY, 2, depth).transpose(0, 2, 1, 3).reshape(TX, TY * depth)


def solution(mesh):
    in_specs = (
        P(("gx", "gy"), None),
        P(),
        P(("gx", "gy"), None),
        P(("gx", "gy"), None),
        P(),
        P(),
        P(),
    )
    return jax.shard_map(
        functools.partial(body, mesh.shape["gx"], mesh.shape["gy"]),
        mesh=mesh,
        in_specs=in_specs,
        out_specs=P("gx", "gy"),
        check_vma=False,
    )
```

time: 124 us -> 46 us (0.37)
  waiting for transfers between devices: 54.9 us -> 0 us
  Pallas kernels: 0 us -> 40.6 us
  matrix products: 32.8 us -> 0 us
  starting transfers between devices: 20.4 us -> 0 us
  other arithmetic: 6.23 us -> 0 us
  local copies, waits for them, and re-layouts: 7.96 us -> 5.03 us
    all_to_all x2 -> x0, waiting for transfers between devices: 49.6 us -> none  [the longest x1 49.6 us: body(): lax.all_to_all(outgoing, ('gx', 'gy'), split_axis=0, concat_axis=0, tiled...]
    pallas_call x0 -> x2, Pallas kernels: none -> 40.6 us  [the longest x1 27.2 us: body(): pl.pallas_call(functools.partial(local_kernel, ngx, ngy), out_shape=jax.S...]
    dot_general x17 -> x0, matrix products: 32.8 us -> none  [the longest x8 19.1 us: add_rows(): jnp.dot(received, weights.reshape(samples, block_bins * depth), preferred...]
    all_to_all x2 -> x0, starting transfers between devices: 13.1 us -> none  [the longest x1 7.3 us: body(): lax.all_to_all(outgoing_pairs, ('gx', 'gy'), split_axis=0, concat_axis=0,...]
    ppermute x4 -> x0, starting transfers between devices: 7.22 us -> none  [the longest x2 4.63 us: with_halo(): lax.ppermute(tail, axis, [(i, (i + 1) % count) for i in range(ends)])]
    ppermute x4 -> x0, waiting for transfers between devices: 5.3 us -> none  [the longest x2 4.5 us: with_halo(): lax.ppermute(head, axis, [((i + 1) % count, i) for i in range(ends)])]
    unnamed x12 -> x19, local copies, waits for them, and re-layouts: 1.06 us -> 3.57 us
    slice x3 -> x0, local copies, waits for them, and re-layouts: 1.84 us -> none  [the longest x1 1.62 us: fir_filter(): filter_taps[offset]]
  transfers between devices with their start and end apart: 6 -> 0, of which waited for: 3 -> 0; matrix products, arithmetic and copies ran while one was open for 9% -> 0% of each run, Pallas kernels for 0% -> 0%
where the time goes in v1:
time: 46 us; the launch traced here: 45.7 us
  Pallas kernels  40.6 us (88%)
  local copies, waits for them, and re-layouts  5.03 us (11%)
    pallas_call x1, Pallas kernels, body(): pl.pallas_call(functools.partial(local_kernel, ngx, ngy), out_shape=jax.S...  27.2 us
    pallas_call x1, Pallas kernels, body(): pl.pallas_call(functools.partial(exchange_kernel, count, ngy), out_shape=...  13.5 us
    unnamed x19, local copies, waits for them, and re-layouts  3.57 us
    reshape x2, local copies, waits for them, and re-layouts, body(): image.reshape(2, TY, 2, depth).transpose(0, 2, 1, 3).reshape(TX, TY * depth)  1.45 us

profile of v1, /device:TPU:0, one launch (start us, length us, event | category | flops | bytes accessed | tf_op | source)
XLA Modules:
  0.0 45.7 jit_solution(12789540886032616161)
XLA Ops:
  0.0 0.0 copy-start.3
  0.0 0.0 copy-start.6
  0.0 0.8 %copy.8.ap_ref = s32[64,8]{1,0:T(8,128)S(1)} copy(s32[64,8]{0,1:T(8,128)} %param.9) | data formatting | bytes 4096 | tf_op args[2]
  0.8 0.0 copy-done.6
  0.8 0.0 copy-start.4
  0.8 0.1 copy.9.mid_ref
  0.9 0.0 copy-done.3
  0.9 0.0 copy-start.1
  0.9 0.1 copy.10.ti_ref
  1.0 0.6 %copy-done.4 = f32[128,64]{0,1:T(8,128)S(1)} copy-done((f32[128,64]{0,1:T(8,128)S(1)}, f32[128,64]{0,1:T(8,128)}, u32[]{:S(2)}) %copy-start.4) | copy-done | bytes 32792
  1.6 0.0 copy-start.5
  1.6 0.1 copy.11.tf_ref
  1.7 0.7 %copy-done.5 = f32[128,64]{0,1:T(8,128)S(1)} copy-done((f32[128,64]{0,1:T(8,128)S(1)}, f32[128,64]{0,1:T(8,128)}, u32[]{:S(2)}) %copy-start.5) | copy-done | bytes 32792
  2.3 0.0 copy-start.2
  2.3 0.1 copy.12.am_ref
  2.4 0.0 copy-done.1
  2.4 0.5 %copy-done.2 = f32[8]{0:T(128)S(1)} copy-done((f32[8]{0:T(128)S(1)}, f32[8]{0:T(128)}, u32[]{:S(2)}) %copy-start.2) | copy-done | bytes 56
  3.0 27.2 %migrate.1.part_ref = bf16[32,16,128]{2,1,0:T(8,128)(2,1)S(1)} custom-call(f32[8]{0:T(128)S(1)} %copy-done.2, s32[64,8]{1,0:T(8,128)S(1)} %copy.8.ap_ref, s32[64,8]{1,0:T(8,128)S(1)} %copy.9.mid_ref, bf16[64,1024]{1,0:T(8,128)(2,1)S(1)} %copy-done.1, s32[128,64]{1,0:T(8,128)S(1)} %copy.10.ti_ref, f32[128,64]{1,0:T(8,128)S(1)} %copy.11.tf_ref, ...), custom_call_target="tpu_custom_call" | custom-call | tf_op jit(solution)/shard_map/migrate/pallas_call | solution.py:200
  30.1 0.0 copy-start
  30.1 0.6 %copy-done = bf16[32,16,128]{2,1,0:T(8,128)(2,1)} copy-done((bf16[32,16,128]{2,1,0:T(8,128)(2,1)}, bf16[32,16,128]{2,1,0:T(8,128)(2,1)S(1)}, u32[]{:S(2)}) %copy-start) | copy-done | bytes 131096
  30.8 13.5 %exchange.1 = f32[16,128]{1,0:T(8,128)} custom-call(bf16[32,16,128]{2,1,0:T(8,128)(2,1)} %copy-done), custom_call_target="tpu_custom_call" | custom-call | tf_op jit(solution)/shard_map/exchange/pallas_call | solution.py:217
  44.2 0.8 %reshape.6 = f32[2,8,2,64]{3,2,1,0:T(2,128)S(1)} reshape(f32[16,128]{1,0:T(8,128)} %exchange.1) | data formatting | bytes 16384 | tf_op jit(solution)/shard_map/reshape | solution.py:230
  45.0 0.7 %reshape.7 = f32[4,512]{1,0:T(4,128)} reshape(f32[2,2,8,64]{3,2,1,0:T(8,128)S(1)} %copy.13) | data formatting | bytes 16384 | tf_op jit(solution)/shard_map/reshape | solution.py:230
  (1 shorter events, 0.0 us)
Async XLA Ops:
  0.0 0.9 %copy-start.3 = (s32[128,64]{0,1:T(8,128)S(1)}, s32[128,64]{0,1:T(8,128)}, u32[]{:S(2)}) copy-start(s32[128,64]{0,1:T(8,128)} %param.11) | copy-start | bytes 98308
  0.0 0.8 %copy-start.6 = (s32[64,8]{0,1:T(8,128)S(1)}, s32[64,8]{0,1:T(8,128)}, u32[]{:S(2)}) copy-start(s32[64,8]{0,1:T(8,128)} %param.10) | copy-start | bytes 6148
  0.8 0.8 %copy-start.4 = (f32[128,64]{0,1:T(8,128)S(1)}, f32[128,64]{0,1:T(8,128)}, u32[]{:S(2)}) copy-start(f32[128,64]{0,1:T(8,128)} %param.12) | copy-start | bytes 98308
  0.9 1.5 %copy-start.1 = (bf16[64,1024]{1,0:T(8,128)(2,1)S(1)}, bf16[64,1024]{1,0:T(8,128)(2,1)}, u32[]{:S(2)}) copy-start(bf16[64,1024]{1,0:T(8,128)(2,1)} %tr_ref.1) | copy-start | bytes 393220
  1.6 0.8 %copy-start.5 = (f32[128,64]{0,1:T(8,128)S(1)}, f32[128,64]{0,1:T(8,128)}, u32[]{:S(2)}) copy-start(f32[128,64]{0,1:T(8,128)} %param.13) | copy-start | bytes 98308
  2.3 0.7 %copy-start.2 = (f32[8]{0:T(128)S(1)}, f32[8]{0:T(128)}, u32[]{:S(2)}) copy-start(f32[8]{0:T(128)} %taps_ref.1) | copy-start | bytes 100
  30.1 0.6 %copy-start = (bf16[32,16,128]{2,1,0:T(8,128)(2,1)}, bf16[32,16,128]{2,1,0:T(8,128)(2,1)S(1)}, u32[]{:S(2)}) copy-start(bf16[32,16,128]{2,1,0:T(8,128)(2,1)S(1)} %migrate.1.part_ref) | copy-start | bytes 393220

commit v2 on v1

--- a/solution.py
+++ b/solution.py
@@ -11,24 +11,55 @@
 TY = 8
 MESH = pl.DeviceIdType.MESH
 WINDOW = 256
-PAIRS = 14
+PAIRS = 7
 FLAT = 32
-STRIDE = PAIRS * FLAT
+PITCH = 72
 
 
 def local_kernel(
-    ngx, ngy, taps_ref, ap_ref, mid_ref, tr_ref, ti_ref, tf_ref, am_ref, out_ref,
-    f4_ref, idx_ref, low_ref, high_ref, amp_ref, tab_ref, img_ref,
+    ngx, ngy, taps_hbm, ap_hbm, mid_hbm, tr_hbm, ti_hbm, tf_hbm, am_hbm, out_ref,
+    taps_ref, ap_ref, mid_ref, tr_ref, ti_ref, tf_ref, am_ref, arrive,
+    f4_ref, idx_ref, low_ref, high_ref, amp_ref, tab_ref, one_ref, two_ref, img_ref,
+    where_ref, spots_ref, moved_sem,
 ):
     f32, bf16 = jnp.float32, jnp.bfloat16
     rows, samples = tr_ref.shape
     taps_count = taps_ref.shape[0]
-    entries = ap_ref.shape[1]
+    entries = ap_ref.shape[0]
     windows = samples // WINDOW
     span = 2 * TY
     cols = idx_ref.shape[1]
     pitch = ngy * TY + 16
-
+    tiles = ngx * ngy
+
+    pairs = [
+        (ap_hbm, ap_ref), (mid_hbm, mid_ref), (taps_hbm, taps_ref), (tr_hbm, tr_ref),
+        (ti_hbm, ti_ref), (tf_hbm, tf_ref), (am_hbm, am_ref),
+    ]
+    copies = [pltpu.make_async_copy(a, b, arrive.at[i]) for i, (a, b) in enumerate(pairs)]
+    for c in copies:
+        c.start()
+    one_ref[...] = jnp.zeros_like(one_ref)
+    two_ref[...] = jnp.zeros_like(two_ref)
+    img_ref[...] = jnp.zeros_like(img_ref)
+
+    copies[0].wait()
+    copies[1].wait()
+    mids = mid_ref[...]
+    tile = ap_ref[...]
+    row = (mids * 2731) >> 16
+    base = 23 - mids + 24 * row
+    for u in range(2):
+        apart = row - 4 - 2 * u
+        near = jnp.maximum(apart, 1 - apart) - 1
+        bank = jnp.where(apart <= 0, 1, 0)
+        where_ref[(2 * u) * entries : (2 * u + 1) * entries, 0:rows] = (near * FLAT + base) * PITCH
+        where_ref[(2 * u + 1) * entries : (2 * u + 2) * entries, 0:rows] = (tile * 4 + bank * 2 + u) * TY
+    moving = pltpu.make_async_copy(where_ref, spots_ref, moved_sem)
+    moving.start()
+
+    copies[2].wait()
+    copies[3].wait()
     x = tr_ref[...].astype(f32)
     lane = lax.broadcasted_iota(jnp.int32, (rows, samples), 1)
     total = jnp.zeros((rows, samples), f32)
@@ -41,12 +72,12 @@
     rounded = filtered.astype(f32)
     edges = [rounded[:, j * WINDOW : j * WINDOW + 1] for j in range(1, windows)]
 
+    for c in copies[4:]:
+        c.wait()
     for m in range(TX):
         def side(ref):
-            return jnp.concatenate(
-                [ref[(2 * m) * span : (2 * m + 1) * span, :], ref[(2 * m + 1) * span : (2 * m + 2) * span, :]],
-                axis=1,
-            )
+            both = ref[:, (2 * m) * span : (2 * m + 2) * span].T
+            return jnp.concatenate([both[:span], both[span:]], axis=1)
 
         here = slice(m * 128, (m + 1) * 128)
         frac = side(tf_ref)
@@ -86,45 +117,50 @@
         value = value + over * edge
         sample = (amp * value).astype(bf16).astype(f32)
         own = [sample[:, m * 128 : (m + 1) * 128] for m in range(TX)]
-        swapped = [pltpu.roll(s, 64, 1) for s in own]
-
-        def put(offset, block):
-            start = (offset + 6) * FLAT + 15
-            tab_ref[pl.ds(start - b, rows, stride=STRIDE), :] = block
-            tab_ref[pl.ds(start + b, rows, stride=STRIDE), :] = block
+
+        def put(far, block):
+            start = (far - 1) * FLAT + 15
+            tab_ref[pl.ds(pl.multiple_of((start - b) * PITCH, 8), rows), :] = block
+            tab_ref[pl.ds(pl.multiple_of((start + b) * PITCH, 8), rows), :] = block
 
         for m in range(TX):
-            put(2 * m + 1, swapped[m])
-            put(-2 * m, own[m])
+            put(2 * m + 1, pltpu.roll(own[m], 64, 1))
             if m < TX - 1:
                 put(2 * m + 2, jnp.where(first, own[m + 1], own[m]))
-                put(-2 * m - 1, jnp.where(first, swapped[m], swapped[m + 1]))
-        return carry
-
-    lax.fori_loop(0, span, per_distance, 0)
-
-    img_ref[...] = jnp.zeros_like(img_ref)
+        return carry
+
+    lax.fori_loop(0, span, per_distance, 0, unroll=16)
+
+    moving.wait()
+    half = rows // 2
 
     def per_trace(t, carry):
-        base = t * STRIDE + 23
-        source, place = [], []
-        for e in range(entries):
-            m = mid_ref[t, e]
-            tile = ap_ref[t, e]
-            source.append(base - m + 56 * ((m * 2731) >> 16))
-            place.append(
-                pl.multiple_of(pitch + 8 + (tile // ngy) * (2 * pitch) + (tile % ngy) * TY, 8)
-            )
-        sums = []
-        for e in range(entries):
-            sums.append(img_ref[pl.ds(place[e], TY), :] + tab_ref[pl.ds(source[e] + 2 * FLAT, TY), :])
-            sums.append(img_ref[pl.ds(place[e] + pitch, TY), :] + tab_ref[pl.ds(source[e], TY), :])
-        for e in range(entries):
-            img_ref[pl.ds(place[e], TY), :] = sums[2 * e]
-            img_ref[pl.ds(place[e] + pitch, TY), :] = sums[2 * e + 1]
-        return carry
-
-    lax.fori_loop(0, rows, per_trace, 0)
+        for into, trace in ((one_ref, t), (two_ref, t + half)):
+            sums = []
+            for e in range(entries):
+                for u in range(2):
+                    source = spots_ref[(2 * u) * entries + e, trace] + trace
+                    place = pl.multiple_of(spots_ref[(2 * u + 1) * entries + e, trace], TY)
+                    sums.append(
+                        (place, into[pl.ds(place, TY), :] + tab_ref[pl.ds(source, TY, stride=PITCH), :])
+                    )
+            for place, value in sums:
+                into[pl.ds(place, TY), :] = value
+        return carry
+
+    lax.fori_loop(0, half, per_trace, 0)
+
+    def gather(tile, carry):
+        spot = pl.multiple_of(pitch + 8 + (tile // ngy) * (2 * pitch) + (tile % ngy) * TY, 8)
+        for u in range(2):
+            plain = pl.multiple_of((tile * 4 + u) * TY, TY)
+            turned = pl.multiple_of((tile * 4 + 2 + u) * TY, TY)
+            img_ref[pl.ds(spot + u * pitch, TY), :] = (
+                one_ref[pl.ds(plain, TY), :] + two_ref[pl.ds(plain, TY), :]
+            ) + pltpu.roll(one_ref[pl.ds(turned, TY), :] + two_ref[pl.ds(turned, TY), :], 64, 1)
+        return carry
+
+    lax.fori_loop(0, tiles, gather, 0, unroll=8)
 
     head = lax.broadcasted_iota(jnp.int32, (TY, 128), 1) < 64
 
@@ -140,10 +176,10 @@
         out_ref[tile] = jnp.concatenate(parts, axis=0).astype(bf16)
         return carry
 
-    lax.fori_loop(0, ngx * ngy, per_tile, 0, unroll=4)
-
-
-def exchange_kernel(count, ngy, part_ref, out_ref, held, send_sem, recv_sem):
+    lax.fori_loop(0, tiles, per_tile, 0, unroll=8)
+
+
+def exchange_kernel(count, ngy, part_ref, out_ref, held, send_sem, recv_sem, own_sem):
     me = lax.axis_index("gx") * ngy + lax.axis_index("gy")
 
     def at(peer):
@@ -174,12 +210,15 @@
         return carry
 
     lax.fori_loop(1, count, send, 0)
+    mine = pltpu.make_async_copy(part_ref.at[me], held.at[0], own_sem)
+    mine.start()
+    mine.wait()
 
     def take(step, total):
         copy(step).wait_recv()
         return total + held[step].astype(jnp.float32)
 
-    total = lax.fori_loop(1, count, take, part_ref[me].astype(jnp.float32))
+    total = lax.fori_loop(1, count, take, held[0].astype(jnp.float32))
     out_ref[...] = total
 
     def done(step, carry):
@@ -196,33 +235,49 @@
     span = 2 * TY
     cols = 2 * TX * depth
     vmem = pl.BlockSpec(memory_space=pltpu.VMEM)
-    smem = pl.BlockSpec(memory_space=pltpu.SMEM)
+    hbm = pl.BlockSpec(memory_space=pltpu.HBM)
+    entries = aperture.shape[1]
+    i32, f32, bf16 = jnp.int32, jnp.float32, jnp.bfloat16
     parts = pl.pallas_call(
         functools.partial(local_kernel, ngx, ngy),
         out_shape=jax.ShapeDtypeStruct((count, 2 * TY, 2 * depth), jnp.bfloat16),
-        in_specs=[smem, smem, smem, vmem, vmem, vmem, vmem],
+        in_specs=[hbm] * 7,
         out_specs=vmem,
         scratch_shapes=[
-            pltpu.VMEM((rows * samples // WINDOW, WINDOW), jnp.bfloat16),
-            pltpu.VMEM((span, cols), jnp.int32),
-            pltpu.VMEM((span, cols), jnp.float32),
-            pltpu.VMEM((span, cols), jnp.float32),
-            pltpu.VMEM((span, cols), jnp.float32),
-            pltpu.VMEM((rows * STRIDE, 2 * depth), jnp.float32),
-            pltpu.VMEM(((2 * ngx + 2) * (ngy * TY + 16), 2 * depth), jnp.float32),
+            pltpu.SMEM(filter_taps.shape, f32),
+            pltpu.VMEM((entries, rows), i32),
+            pltpu.VMEM((entries, rows), i32),
+            pltpu.VMEM((rows, samples), bf16),
+            pltpu.VMEM(time_index.shape[::-1], i32),
+            pltpu.VMEM(time_index.shape[::-1], f32),
+            pltpu.VMEM(time_index.shape[::-1], f32),
+            pltpu.SemaphoreType.DMA((7,)),
+            pltpu.VMEM((rows * samples // WINDOW, WINDOW), bf16),
+            pltpu.VMEM((span, cols), i32),
+            pltpu.VMEM((span, cols), f32),
+            pltpu.VMEM((span, cols), f32),
+            pltpu.VMEM((span, cols), f32),
+            pltpu.VMEM((PAIRS * FLAT * PITCH, 2 * depth), f32),
+            pltpu.VMEM((count * 4 * TY, 2 * depth), f32),
+            pltpu.VMEM((count * 4 * TY, 2 * depth), f32),
+            pltpu.VMEM(((2 * ngx + 2) * (ngy * TY + 16), 2 * depth), f32),
+            pltpu.VMEM((4 * entries, 128), i32),
+            pltpu.SMEM((4 * entries, 128), i32),
+            pltpu.SemaphoreType.DMA,
         ],
         compiler_params=pltpu.CompilerParams(vmem_limit_bytes=40 * 1024 * 1024),
         name="migrate",
-    )(filter_taps, aperture, midpoint, traces, time_index, time_frac, amplitude)
+    )(filter_taps, aperture.T, midpoint.T, traces, time_index.T, time_frac.T, amplitude.T)
     image = pl.pallas_call(
         functools.partial(exchange_kernel, count, ngy),
         out_shape=jax.ShapeDtypeStruct((2 * TY, 2 * depth), jnp.float32),
-        in_specs=[vmem],
+        in_specs=[pl.BlockSpec(memory_space=pl.ANY)],
         out_specs=vmem,
         scratch_shapes=[
             pltpu.VMEM((count, 2 * TY, 2 * depth), jnp.bfloat16),
             pltpu.SemaphoreType.DMA((count,)),
             pltpu.SemaphoreType.DMA((count,)),
+            pltpu.SemaphoreType.DMA,
         ],
         compiler_params=pltpu.CompilerParams(collective_id=0, has_side_effects=True),
         name="exchange",

time: 46 us -> 26.9 us (0.58)
  Pallas kernels: 40.6 us -> 20.5 us
  local copies, waits for them, and re-layouts: 5.03 us -> 5.98 us
    pallas_call x1, Pallas kernels: 27.2 us -> 7.7 us  [body(): pl.pallas_call(functools.partial(local_kernel, ngx, ngy), out_shape=jax.S...]
    unnamed x19 -> x16, local copies, waits for them, and re-layouts: 3.57 us -> 4.52 us
    pallas_call x1, Pallas kernels: 13.5 us -> 12.8 us  [body(): pl.pallas_call(functools.partial(exchange_kernel, count, ngy), out_shape=...]
where the time goes in v2:
time: 26.9 us; the launch traced here: 26.5 us
  Pallas kernels  20.5 us (76%)
  local copies, waits for them, and re-layouts  5.98 us (22%)
    pallas_call x1, Pallas kernels, body(): pl.pallas_call(functools.partial(exchange_kernel, count, ngy), out_shape=...  12.8 us
    pallas_call x1, Pallas kernels, body(): pl.pallas_call(functools.partial(local_kernel, ngx, ngy), out_shape=jax.S...  7.7 us
    unnamed x16, local copies, waits for them, and re-layouts  4.52 us
    reshape x2, local copies, waits for them, and re-layouts, body(): image.reshape(2, TY, 2, depth).transpose(0, 2, 1, 3).reshape(TX, TY * depth)  1.45 us

profile of v2, /device:TPU:0, one launch (start us, length us, event | category | flops | bytes accessed | tf_op | source)
XLA Modules:
  0.0 26.5 jit_solution(2326818607737413991)
XLA Ops:
  0.0 0.0 copy-start.6
  0.0 0.0 copy-start.5
  0.0 0.0 copy-start.7
  0.0 0.7 %copy-done.6 = s32[64,8]{0,1:T(8,128)S(1)} copy-done((s32[64,8]{0,1:T(8,128)S(1)}, s32[64,8]{0,1:T(8,128)}, u32[]{:S(2)}) %copy-start.6) | copy-done | bytes 2072
  0.7 0.0 copy-done.5
  0.7 0.0 copy-done.7
  0.7 0.0 copy-start.1
  0.7 0.9 %copy-done.1 = bf16[64,1024]{1,0:T(8,128)(2,1)S(1)} copy-done((bf16[64,1024]{1,0:T(8,128)(2,1)S(1)}, bf16[64,1024]{1,0:T(8,128)(2,1)}, u32[]{:S(2)}) %copy-start.1) | copy-done | bytes 131096
  1.6 0.0 copy-start.2
  1.6 0.8 %copy-done.2 = s32[128,64]{0,1:T(8,128)S(1)} copy-done((s32[128,64]{0,1:T(8,128)S(1)}, s32[128,64]{0,1:T(8,128)}, u32[]{:S(2)}) %copy-start.2) | copy-done | bytes 32792
  2.4 0.0 copy-start.3
  2.4 0.8 %copy-done.3 = f32[128,64]{0,1:T(8,128)S(1)} copy-done((f32[128,64]{0,1:T(8,128)S(1)}, f32[128,64]{0,1:T(8,128)}, u32[]{:S(2)}) %copy-start.3) | copy-done | bytes 32792
  3.1 0.0 copy-start.4
  3.1 0.8 %copy-done.4 = f32[128,64]{0,1:T(8,128)S(1)} copy-done((f32[128,64]{0,1:T(8,128)S(1)}, f32[128,64]{0,1:T(8,128)}, u32[]{:S(2)}) %copy-start.4) | copy-done | bytes 32792
  3.9 7.7 %migrate.1.part_ref = bf16[32,16,128]{2,1,0:T(8,128)(2,1)S(1)} custom-call(f32[8]{0:T(128)S(1)} %copy-done.7, s32[8,64]{1,0:T(8,128)S(1)} %bitcast.11, s32[8,64]{1,0:T(8,128)S(1)} %bitcast.12, bf16[64,1024]{1,0:T(8,128)(2,1)S(1)} %copy-done.1, s32[64,128]{1,0:T(8,128)S(1)} %bitcast.8, f32[64,128]{1,0:T(8,128)S(1)} %bitcast.9, f32[64,128]{1,0:T(8,128)S(1)} %bitcast.10), custom_call_target="tpu_custom_call" | custom-call | tf_op jit(solution)/shard_map/migrate/pallas_call | solution.py:241
  11.6 0.0 copy-start
  11.6 0.6 %copy-done = bf16[32,16,128]{2,1,0:T(8,128)(2,1)} copy-done((bf16[32,16,128]{2,1,0:T(8,128)(2,1)}, bf16[32,16,128]{2,1,0:T(8,128)(2,1)S(1)}, u32[]{:S(2)}) %copy-start) | copy-done | bytes 131096
  12.2 12.8 %exchange.1 = f32[16,128]{1,0:T(8,128)} custom-call(bf16[32,16,128]{2,1,0:T(8,128)(2,1)} %copy-done), custom_call_target="tpu_custom_call" | custom-call | tf_op jit(solution)/shard_map/exchange/pallas_call | solution.py:271
  25.0 0.8 %reshape.6 = f32[2,8,2,64]{3,2,1,0:T(2,128)S(1)} reshape(f32[16,128]{1,0:T(8,128)} %exchange.1) | data formatting | bytes 16384 | tf_op jit(solution)/shard_map/reshape | solution.py:285
  25.8 0.7 %reshape.7 = f32[4,512]{1,0:T(4,128)} reshape(f32[2,2,8,64]{3,2,1,0:T(8,128)S(1)} %copy.8) | data formatting | bytes 16384 | tf_op jit(solution)/shard_map/reshape | solution.py:285
  (1 shorter events, 0.0 us)
Async XLA Ops:
  0.0 0.7 %copy-start.6 = (s32[64,8]{0,1:T(8,128)S(1)}, s32[64,8]{0,1:T(8,128)}, u32[]{:S(2)}) copy-start(s32[64,8]{0,1:T(8,128)} %param.10) | copy-start | bytes 6148
  0.0 0.7 %copy-start.5 = (s32[64,8]{0,1:T(8,128)S(1)}, s32[64,8]{0,1:T(8,128)}, u32[]{:S(2)}) copy-start(s32[64,8]{0,1:T(8,128)} %param.9) | copy-start | bytes 6148
  0.0 0.7 %copy-start.7 = (f32[8]{0:T(128)S(1)}, f32[8]{0:T(128)}, u32[]{:S(2)}) copy-start(f32[8]{0:T(128)} %taps_hbm.1) | copy-start | bytes 100
  0.7 0.9 %copy-start.1 = (bf16[64,1024]{1,0:T(8,128)(2,1)S(1)}, bf16[64,1024]{1,0:T(8,128)(2,1)}, u32[]{:S(2)}) copy-start(bf16[64,1024]{1,0:T(8,128)(2,1)} %tr_hbm.1) | copy-start | bytes 393220
  1.6 0.8 %copy-start.2 = (s32[128,64]{0,1:T(8,128)S(1)}, s32[128,64]{0,1:T(8,128)}, u32[]{:S(2)}) copy-start(s32[128,64]{0,1:T(8,128)} %param.11) | copy-start | bytes 98308
  2.4 0.8 %copy-start.3 = (f32[128,64]{0,1:T(8,128)S(1)}, f32[128,64]{0,1:T(8,128)}, u32[]{:S(2)}) copy-start(f32[128,64]{0,1:T(8,128)} %param.12) | copy-start | bytes 98308
  3.1 0.8 %copy-start.4 = (f32[128,64]{0,1:T(8,128)S(1)}, f32[128,64]{0,1:T(8,128)}, u32[]{:S(2)}) copy-start(f32[128,64]{0,1:T(8,128)} %param.13) | copy-start | bytes 98308
  11.6 0.7 %copy-start = (bf16[32,16,128]{2,1,0:T(8,128)(2,1)}, bf16[32,16,128]{2,1,0:T(8,128)(2,1)S(1)}, u32[]{:S(2)}) copy-start(bf16[32,16,128]{2,1,0:T(8,128)(2,1)S(1)} %migrate.1.part_ref) | copy-start | bytes 393220

commit v3 on v2

--- a/solution.py
+++ b/solution.py
@@ -8,12 +8,14 @@
 from jax.sharding import PartitionSpec as P
 
 TX = 4
+LIMIT1 = 63 * 1024 * 1024
+LIMIT2 = 16 * 1024 * 1024
 TY = 8
 MESH = pl.DeviceIdType.MESH
 WINDOW = 256
 PAIRS = 7
 FLAT = 32
-PITCH = 72
+PITCH = 8
 
 
 def local_kernel(
@@ -49,11 +51,14 @@
     tile = ap_ref[...]
     row = (mids * 2731) >> 16
     base = 23 - mids + 24 * row
+    trace = lax.broadcasted_iota(jnp.int32, (entries, rows), 1)
     for u in range(2):
         apart = row - 4 - 2 * u
         near = jnp.maximum(apart, 1 - apart) - 1
         bank = jnp.where(apart <= 0, 1, 0)
-        where_ref[(2 * u) * entries : (2 * u + 1) * entries, 0:rows] = (near * FLAT + base) * PITCH
+        where_ref[(2 * u) * entries : (2 * u + 1) * entries, 0:rows] = (
+            (near * (rows // 8) + (trace >> 3)) * FLAT + base
+        ) * PITCH + (trace & 7)
         where_ref[(2 * u + 1) * entries : (2 * u + 2) * entries, 0:rows] = (tile * 4 + bank * 2 + u) * TY
     moving = pltpu.make_async_copy(where_ref, spots_ref, moved_sem)
     moving.start()
@@ -119,9 +124,11 @@
         own = [sample[:, m * 128 : (m + 1) * 128] for m in range(TX)]
 
         def put(far, block):
-            start = (far - 1) * FLAT + 15
-            tab_ref[pl.ds(pl.multiple_of((start - b) * PITCH, 8), rows), :] = block
-            tab_ref[pl.ds(pl.multiple_of((start + b) * PITCH, 8), rows), :] = block
+            for g in range(rows // 8):
+                start = ((far - 1) * (rows // 8) + g) * FLAT + 15
+                part = block[8 * g : 8 * g + 8]
+                tab_ref[pl.ds((start - b) * PITCH, 8), :] = part
+                tab_ref[pl.ds((start + b) * PITCH, 8), :] = part
 
         for m in range(TX):
             put(2 * m + 1, pltpu.roll(own[m], 64, 1))
@@ -139,7 +146,7 @@
             sums = []
             for e in range(entries):
                 for u in range(2):
-                    source = spots_ref[(2 * u) * entries + e, trace] + trace
+                    source = spots_ref[(2 * u) * entries + e, trace]
                     place = pl.multiple_of(spots_ref[(2 * u + 1) * entries + e, trace], TY)
                     sums.append(
                         (place, into[pl.ds(place, TY), :] + tab_ref[pl.ds(source, TY, stride=PITCH), :])
@@ -173,59 +180,93 @@
             along = img_ref[pl.ds(start + u * pitch - 1, TY), :] + img_ref[pl.ds(start + u * pitch + 1, TY), :]
             across = pltpu.roll(jnp.where(head, above + mid, mid + below), 64, 1)
             parts.append(mid + 0.25 * (across + along))
-        out_ref[tile] = jnp.concatenate(parts, axis=0).astype(bf16)
+        a, b = tile // ngy, tile % ngy
+        out_ref[b % 2, a * (ngy // 2) + b // 2] = jnp.concatenate(parts, axis=0).astype(bf16)
         return carry
 
     lax.fori_loop(0, tiles, per_tile, 0, unroll=8)
 
 
-def exchange_kernel(count, ngy, part_ref, out_ref, held, send_sem, recv_sem, own_sem):
-    me = lax.axis_index("gx") * ngy + lax.axis_index("gy")
-
-    def at(peer):
-        return (peer // ngy, peer % ngy)
+def exchange_kernel(
+    half, part_ref, out_ref, own, near, both, held, own_sem, near_send, near_recv, send_sem, recv_sem
+):
+    x, y = lax.axis_index("gx"), lax.axis_index("gy")
+    cross = lax.axis_size("gy") // 2
+    core = y % 2
+    spot = x * cross + y // 2
+    twin = (x, y + 1 - 2 * core)
+
+    def at(step):
+        peer = (spot + step) % half
+        return (peer // cross, (peer % cross) * 2 + core)
 
     barrier = pltpu.get_barrier_semaphore()
+    pl.semaphore_signal(barrier, inc=1, device_id=twin, device_id_type=MESH)
 
     def greet(step, carry):
-        pl.semaphore_signal(barrier, inc=1, device_id=at((me + step) % count), device_id_type=MESH)
-        return carry
-
-    lax.fori_loop(1, count, greet, 0)
-    pl.semaphore_wait(barrier, count - 1)
+        pl.semaphore_signal(barrier, inc=1, device_id=at(step), device_id_type=MESH)
+        return carry
+
+    lax.fori_loop(1, half, greet, 0, unroll=True)
+    mine = pltpu.make_async_copy(part_ref.at[core], own, own_sem)
+    mine.start()
+    pl.semaphore_wait(barrier, half)
+
+    swap = pltpu.make_async_remote_copy(
+        src_ref=part_ref.at[1 - core],
+        dst_ref=near,
+        send_sem=near_send,
+        recv_sem=near_recv,
+        device_id=twin,
+        device_id_type=MESH,
+    )
+    swap.start()
+    mine.wait()
+    swap.wait_recv()
+
+    def summed(step):
+        peer = (spot + step) % half
+        return own[peer].astype(jnp.float32) + near[peer].astype(jnp.float32)
 
     def copy(step):
-        peer = (me + step) % count
         return pltpu.make_async_remote_copy(
-            src_ref=part_ref.at[peer],
+            src_ref=both.at[step],
             dst_ref=held.at[step],
             send_sem=send_sem.at[step],
             recv_sem=recv_sem.at[step],
-            device_id=at(peer),
+            device_id=at(step),
             device_id_type=MESH,
         )
 
     def send(step, carry):
+        both[step] = summed(step).astype(jnp.bfloat16)
         copy(step).start()
         return carry
 
-    lax.fori_loop(1, count, send, 0)
-    mine = pltpu.make_async_copy(part_ref.at[me], held.at[0], own_sem)
-    mine.start()
-    mine.wait()
+    lax.fori_loop(1, half, send, 0, unroll=True)
 
     def take(step, total):
         copy(step).wait_recv()
         return total + held[step].astype(jnp.float32)
 
-    total = lax.fori_loop(1, count, take, held[0].astype(jnp.float32))
-    out_ref[...] = total
+    total = lax.fori_loop(1, half, take, summed(0), unroll=True)
+    first = lax.broadcasted_iota(jnp.int32, (1, 128), 1) < 64
+    turned = pltpu.roll(total, 64, 1)
+    for u in range(2):
+        for w in range(TY // 2):
+            even = slice(u * TY + 2 * w, u * TY + 2 * w + 1)
+            odd = slice(u * TY + 2 * w + 1, u * TY + 2 * w + 2)
+            here = slice(w * 128, (w + 1) * 128)
+            out_ref[2 * u : 2 * u + 1, here] = jnp.where(first, total[even], turned[odd])
+            out_ref[2 * u + 1 : 2 * u + 2, here] = jnp.where(first, turned[even], total[odd])
+
+    swap.wait_send()
 
     def done(step, carry):
         copy(step).wait_send()
         return carry
 
-    lax.fori_loop(1, count, done, 0)
+    lax.fori_loop(1, half, done, 0, unroll=True)
 
 
 def body(ngx, ngy, traces, filter_taps, aperture, midpoint, time_index, time_frac, amplitude):
@@ -240,7 +281,7 @@
     i32, f32, bf16 = jnp.int32, jnp.float32, jnp.bfloat16
     parts = pl.pallas_call(
         functools.partial(local_kernel, ngx, ngy),
-        out_shape=jax.ShapeDtypeStruct((count, 2 * TY, 2 * depth), jnp.bfloat16),
+        out_shape=jax.ShapeDtypeStruct((2, count // 2, 2 * TY, 2 * depth), jnp.bfloat16),
         in_specs=[hbm] * 7,
         out_specs=vmem,
         scratch_shapes=[
@@ -257,7 +298,7 @@
             pltpu.VMEM((span, cols), f32),
             pltpu.VMEM((span, cols), f32),
             pltpu.VMEM((span, cols), f32),
-            pltpu.VMEM((PAIRS * FLAT * PITCH, 2 * depth), f32),
+            pltpu.VMEM((PAIRS * (rows // 8) * FLAT * PITCH, 2 * depth), f32),
             pltpu.VMEM((count * 4 * TY, 2 * depth), f32),
             pltpu.VMEM((count * 4 * TY, 2 * depth), f32),
             pltpu.VMEM(((2 * ngx + 2) * (ngy * TY + 16), 2 * depth), f32),
@@ -265,24 +306,23 @@
             pltpu.SMEM((4 * entries, 128), i32),
             pltpu.SemaphoreType.DMA,
         ],
-        compiler_params=pltpu.CompilerParams(vmem_limit_bytes=40 * 1024 * 1024),
+        compiler_params=pltpu.CompilerParams(vmem_limit_bytes=LIMIT1),
         name="migrate",
     )(filter_taps, aperture.T, midpoint.T, traces, time_index.T, time_frac.T, amplitude.T)
     image = pl.pallas_call(
-        functools.partial(exchange_kernel, count, ngy),
-        out_shape=jax.ShapeDtypeStruct((2 * TY, 2 * depth), jnp.float32),
+        functools.partial(exchange_kernel, count // 2),
+        out_shape=jax.ShapeDtypeStruct((TX, TY * depth), jnp.float32),
         in_specs=[pl.BlockSpec(memory_space=pl.ANY)],
         out_specs=vmem,
         scratch_shapes=[
-            pltpu.VMEM((count, 2 * TY, 2 * depth), jnp.bfloat16),
-            pltpu.SemaphoreType.DMA((count,)),
-            pltpu.SemaphoreType.DMA((count,)),
-            pltpu.SemaphoreType.DMA,
+            *[pltpu.VMEM((count // 2, 2 * TY, 2 * depth), bf16)] * 4,
+            *[pltpu.SemaphoreType.DMA] * 3,
+            *[pltpu.SemaphoreType.DMA((count // 2,))] * 2,
         ],
-        compiler_params=pltpu.CompilerParams(collective_id=0, has_side_effects=True),
+        compiler_params=pltpu.CompilerParams(collective_id=0, has_side_effects=True, vmem_limit_bytes=LIMIT2),
         name="exchange",
     )(parts)
-    return image.reshape(2, TY, 2, depth).transpose(0, 2, 1, 3).reshape(TX, TY * depth)
+    return image
 
 
 def solution(mesh):

time: 26.9 us -> 21.4 us (0.80)
  local copies, waits for them, and re-layouts: 5.98 us -> 1.5 us
  Pallas kernels: 20.5 us -> 19.7 us
    unnamed x16 -> x3, local copies, waits for them, and re-layouts: 4.52 us -> 1.5 us
    pallas_call x1, Pallas kernels: 12.8 us -> 11 us  [body(): pl.pallas_call(functools.partial(exchange_kernel, count // 2), out_shape=...]
    reshape x2 -> x0, local copies, waits for them, and re-layouts: 1.45 us -> none  [body(): image.reshape(2, TY, 2, depth).transpose(0, 2, 1, 3).reshape(TX, TY * depth)]
    pallas_call x1, Pallas kernels: 7.7 us -> 8.71 us  [body(): pl.pallas_call(functools.partial(local_kernel, ngx, ngy), out_shape=jax.S...]
where the time goes in v3:
time: 21.4 us; the launch traced here: 21.2 us
  Pallas kernels  19.7 us (92%)
  local copies, waits for them, and re-layouts  1.5 us (7%)
    pallas_call x1, Pallas kernels, body(): pl.pallas_call(functools.partial(exchange_kernel, count // 2), out_shape=...  11 us
    pallas_call x1, Pallas kernels, body(): pl.pallas_call(functools.partial(local_kernel, ngx, ngy), out_shape=jax.S...  8.71 us
    unnamed x3, local copies, waits for them, and re-layouts  1.5 us

profile of v3, /device:TPU:0, one launch (start us, length us, event | category | flops | bytes accessed | tf_op | source)
XLA Modules:
  0.0 21.2 jit_solution(16664855188075914622)
XLA Ops:
  0.0 8.7 %migrate.1.part_ref = bf16[2,16,16,128]{3,2,1,0:T(8,128)(2,1)} custom-call(f32[8]{0:T(128)} %taps_hbm.1, s32[8,64]{1,0:T(8,128)} %bitcast.8, s32[8,64]{1,0:T(8,128)} %bitcast.9, bf16[64,1024]{1,0:T(8,128)(2,1)} %tr_hbm.1, s32[64,128]{1,0:T(8,128)} %bitcast.5, f32[64,128]{1,0:T(8,128)} %bitcast.6, f32[64,128]{1,0:T(8,128)} %bitcast.7), custom_call_target="tpu_custom_call" | custom-call | tf_op jit(solution)/shard_map/migrate/pallas_call | solution.py:282
  8.7 0.0 copy-start
  8.7 0.9 %copy-done = bf16[2,16,16,128]{3,2,1,0:T(8,128)(2,1)S(1)} copy-done((bf16[2,16,16,128]{3,2,1,0:T(8,128)(2,1)S(1)}, bf16[2,16,16,128]{3,2,1,0:T(8,128)(2,1)}, u32[]{:S(2)}) %copy-start) | copy-done | bytes 131096
  9.6 11.0 %exchange.1 = f32[4,512]{1,0:T(4,128)S(1)} custom-call(bf16[2,16,16,128]{3,2,1,0:T(8,128)(2,1)S(1)} %copy-done), custom_call_target="tpu_custom_call" | custom-call | tf_op jit(solution)/shard_map/exchange/pallas_call | solution.py:312
  20.6 0.6 %copy.9 = f32[4,512]{1,0:T(4,128)} copy(f32[4,512]{1,0:T(4,128)S(1)} %exchange.1) | data formatting | bytes 16384
Async XLA Ops:
  8.7 0.9 %copy-start = (bf16[2,16,16,128]{3,2,1,0:T(8,128)(2,1)S(1)}, bf16[2,16,16,128]{3,2,1,0:T(8,128)(2,1)}, u32[]{:S(2)}) copy-start(bf16[2,16,16,128]{3,2,1,0:T(8,128)(2,1)} %migrate.1.part_ref) | copy-start | bytes 393220
